TPU v7x, 32 devices: a whole 2x2x4 slice. The times are simulated.
32 devices in a mesh: dp: 4 (over y, core), expert: 2 (over x), tensor: 4 (over z).
Axes of the slice: x: 2, y: 2, z: 4, core: 2. Of those that a mesh axis runs over, the one named last changes fastest.
Arguments:
- tokens: bfloat16 [1024, 2048], P(('dp', 'expert')), may hold values from -6 to 6
- cotangent: bfloat16 [1024, 2048], P(('dp', 'expert')), may hold values from -6 to 6
- expert_ids: int32 [1024, 1], P(('dp', 'expert')), may hold values from 0 to 31; in each aligned block of 128 rows (0 to 127, 128 to 255, ...) at most 8 rows name the same one
- gate_weight: bfloat16 [32, 2048, 1408], P('expert', 'dp', 'tensor'), may hold values from -0.125 to 0.125
- up_weight: bfloat16 [32, 2048, 1408], P('expert', 'dp', 'tensor'), may hold values from -0.125 to 0.125
- down_weight: bfloat16 [32, 2048, 1408], P('expert', 'dp', 'tensor'), may hold values from -0.15625 to 0.15625
Outputs:
- grad_tokens: bfloat16 [1024, 2048], P(('dp', 'expert'), 'tensor')
- grad_gate: bfloat16 [32, 2048, 1408], P('expert', 'dp', 'tensor')
- grad_up: bfloat16 [32, 2048, 1408], P('expert', 'dp', 'tensor')
Inputs may be any that keep to these rules, and one draw needn't show every extreme that they name: `expert_ids`: among the 128 tokens of one block no expert id occurs more than 8 times, and in every draw some block holds some id exactly 8 times.
All inputs are finite; a program needn't handle non-finite values.
Results may differ from a plain program's by a relative error of at most 0.013.
Values may be sent and summed in bfloat16 or wider, within the bound.
No kernel may reach another device: no remote copies, remote signals or barrier semaphores. Data moves between devices by JAX's collectives and lax.ppermute only.
A program may use at most 192 MiB of HBM per device.

v0:
```python
import functools

import jax
import jax.numpy as jnp
from jax import lax
from jax.experimental import pallas as pl
from jax.experimental.pallas import tpu as pltpu
from jax.sharding import PartitionSpec as P

CAP = 8
META = 16
F32 = jnp.float32
BF16 = jnp.bfloat16
MIB = 1024 * 1024
PLACE_COST = 1 << 34


def swap(value, axis, count, bit):
    return lax.ppermute(value, axis, [(i, i ^ bit) for i in range(count)])


def whole_spec(shape):
    return pl.BlockSpec(shape, lambda *_: (0,) * len(shape))


def params(mib=16):
    return pltpu.CompilerParams(vmem_limit_bytes=mib * MIB)


def split_kernel(width, n_dp, where, ids, tokens, *refs):
    outs, (meta, sems) = refs[:-2], refs[-2:]
    k, x = where[0], where[1]
    rows = tokens.shape[0]
    copies = []
    for rel in range(n_dp):
        start = pl.multiple_of((k ^ rel) * width, 128)
        copy = pltpu.make_async_copy(
            tokens.at[:, pl.ds(start, width)], outs[rel].at[pl.ds(0, rows), :], sems.at[rel]
        )
        copy.start()
        copies.append(copy)
    along = ids[...].astype(F32)
    line = lax.broadcasted_iota(jnp.int32, (rows, rows), 0)
    lane = lax.broadcasted_iota(jnp.int32, (rows, rows), 1)
    named = jnp.broadcast_to(along, (rows, rows))
    down = jnp.sum(jnp.where(line == lane, named, 0.0), axis=1, keepdims=True)
    earlier = jnp.where((named == down) & (line < lane), 1.0, 0.0)
    place = jnp.sum(earlier, axis=0, keepdims=True) + (x * CAP).astype(F32)
    at = lax.broadcasted_iota(jnp.int32, (META, rows), 0)
    meta[...] = jnp.zeros(meta.shape, BF16)
    meta[:, 0:rows] = jnp.where(at == 0, along, jnp.where(at == 1, place, 0.0)).astype(BF16)
    for rel in range(n_dp):
        copy = pltpu.make_async_copy(meta, outs[rel].at[pl.ds(rows, META), :], sems.at[n_dp + rel])
        copy.start()
        copies.append(copy)
    for copy in copies:
        copy.wait()


def split(where, ids, tokens, width, n_dp):
    rows = tokens.shape[0]
    anywhere = pl.BlockSpec(memory_space=pl.ANY)
    return pl.pallas_call(
        functools.partial(split_kernel, width, n_dp),
        out_shape=[jax.ShapeDtypeStruct((rows + META, width), BF16)] * n_dp,
        in_specs=[
            pl.BlockSpec(memory_space=pltpu.SMEM),
            pl.BlockSpec(memory_space=pltpu.VMEM),
            anywhere,
        ],
        out_specs=[anywhere] * n_dp,
        scratch_shapes=[pltpu.VMEM((META, width), BF16), pltpu.SemaphoreType.DMA((2 * n_dp,))],
        compiler_params=params(),
    )(where, ids, tokens)


def placer_of(row, slot_count):
    every = lax.broadcasted_iota(jnp.int32, (slot_count, row.shape[1]), 0)
    return (every == row).astype(F32).astype(BF16)


def place_kernel(first, rows, where, mine, others, *refs):
    n_dp = len(mine)
    other = []
    for group in others:
        other += [group] if len(group.shape) == 2 else [group.at[i] for i in range(group.shape[0])]
    if first:
        placed, lines = refs[-2:]
    else:
        lines, placed = refs[0], refs[-1]
    local_experts, slot_rows, width = placed.shape
    slots = slot_rows // n_dp
    for rel in range(n_dp):
        if first:
            pair = [b[0 : rows + META, :] for b in (mine[rel], other[rel])]
            metas = [b[rows:, 0:rows].astype(F32) for b in pair]
            ids = jnp.concatenate([m[0:1] for m in metas], axis=1)
            place = jnp.concatenate([m[1:2] for m in metas], axis=1)
            low = (where[1] * local_experts).astype(F32)
            row = ((ids - low) * slots + place).astype(jnp.int32)
            lines[rel] = jnp.broadcast_to(row, (8, row.shape[1]))
            pair = [b[0:rows] for b in pair]
        else:
            row = lines[rel][0:1]
            pair = [b[...] for b in (mine[rel], other[rel])]
        placer = placer_of(row, local_experts * slots)
        found = jnp.dot(placer, jnp.concatenate(pair, axis=0), preferred_element_type=F32).astype(BF16)
        placed[:, rel * slots : (rel + 1) * slots, :] = found.reshape(local_experts, slots, width)


def place(where, mine, others, lines, rows, local_experts, after):
    first = lines is None
    n_dp, slots = len(mine), 2 * CAP
    width = mine[0].shape[1]
    placed = jax.ShapeDtypeStruct((local_experts, n_dp * slots, width), BF16)
    line = jax.ShapeDtypeStruct((n_dp, 8, 2 * rows), jnp.int32)
    vmem = pl.BlockSpec(memory_space=pltpu.VMEM)
    operands = [*others] + ([] if first else [lines])

    def kernel(where, *refs):
        split_at = n_dp + len(others)
        place_kernel(first, rows, where, refs[:n_dp], refs[n_dp:split_at], *refs[split_at:])

    return pl.pallas_call(
        kernel,
        out_shape=[placed, line] if first else placed,
        in_specs=[pl.BlockSpec(memory_space=pltpu.SMEM)]
        + [vmem] * (n_dp + len(operands))
        + [pl.BlockSpec(memory_space=pl.ANY)] * len(after),
        out_specs=[vmem, vmem] if first else vmem,
        compiler_params=params(),
        cost_estimate=pl.CostEstimate(flops=PLACE_COST, bytes_accessed=4 * rows * width * n_dp, transcendentals=0),
    )(where, *mine, *operands, *after)


def back_kernel(rels, lines, h0, h1, gate, up, own0, own1, other0, other1, near, held, sems):
    parts = (h0, h1)
    local_experts, slots, _ = h0.shape
    hidden = gate.shape[1]
    per_copy = local_experts // sems.shape[1]

    def copy_of(which, at):
        group = pl.ds(at * per_copy, per_copy)
        rows = pl.ds(which * hidden, hidden)
        return pltpu.make_async_copy((gate, up)[which].at[group], near.at[group, rows], sems.at[which, at])

    for at in range(sems.shape[1]):
        for which in range(2):
            copy_of(which, at).start()
    for at in range(sems.shape[1]):
        for which in range(2):
            copy_of(which, at).wait()
        for e in range(at * per_copy, (at + 1) * per_copy):
            grads = jnp.concatenate([h[e] for h in parts], axis=0)
            value = jnp.dot(grads, near[e], preferred_element_type=F32).astype(BF16)
            for i in range(2):
                held[i, e * slots : (e + 1) * slots, :] = value[i * slots : (i + 1) * slots]

    rows = own0.shape[0]
    for i, (own, other) in enumerate(((own0, other0), (own1, other1))):
        placer = placer_of(lines[rels[i]][0:1], held.shape[1])
        token_rows = lax.dot_general(
            placer, held[i], (((0,), (0,)), ((), ())), preferred_element_type=F32
        ).astype(BF16)
        own[...] = token_rows[0:rows]
        other[...] = token_rows[rows:]


def back(rels, lines, parts, gate, up, rows):
    local_experts, hidden, width = gate.shape
    slots = parts[0].shape[1]
    vmem = pl.BlockSpec(memory_space=pltpu.VMEM)
    flops = 4 * local_experts * 2 * slots * width * hidden
    return pl.pallas_call(
        functools.partial(back_kernel, rels),
        out_shape=[jax.ShapeDtypeStruct((rows, width), BF16)] * 4,
        in_specs=[vmem] * 3 + [pl.BlockSpec(memory_space=pl.ANY)] * 2,
        out_specs=[vmem] * 4,
        scratch_shapes=[
            pltpu.VMEM((local_experts, 2 * hidden, width), BF16),
            pltpu.VMEM((2, local_experts * slots, width), BF16),
            pltpu.SemaphoreType.DMA((2, 8 if local_experts % 8 == 0 else 1)),
        ],
        compiler_params=params(48),
        cost_estimate=pl.CostEstimate(
            flops=4 * flops, bytes_accessed=2 * local_experts * width * hidden * 2, transcendentals=0
        ),
    )(lines, *parts, gate, up)


def weight_kernel(placed, h0, h1, h2, h3, gate, up):
    hidden = gate.shape[1]
    for i in range(gate.shape[0]):
        grads = jnp.concatenate([h[i] for h in (h0, h1, h2, h3)], axis=0)
        both = lax.dot_general(
            grads, placed[i], (((0,), (0,)), ((), ())), preferred_element_type=F32
        ).astype(BF16)
        gate[i] = both[0:hidden]
        up[i] = both[hidden:]


def weight_grads(placed, parts, per_step):
    local_experts, slot_rows, width = placed.shape
    _, slots, both = parts[0].shape
    hidden = both // 2
    part_spec = pl.BlockSpec((per_step, slots, both), lambda e: (e, 0, 0))
    out_spec = pl.BlockSpec((per_step, hidden, width), lambda e: (e, 0, 0))
    flops = 2 * local_experts * slot_rows * width * both
    return pl.pallas_call(
        weight_kernel,
        grid=(local_experts // per_step,),
        out_shape=[jax.ShapeDtypeStruct((local_experts, hidden, width), BF16)] * 2,
        in_specs=[pl.BlockSpec((per_step, slot_rows, width), lambda e: (e, 0, 0))] + [part_spec] * len(parts),
        out_specs=[out_spec] * 2,
        compiler_params=params(24),
        cost_estimate=pl.CostEstimate(
            flops=4 * flops, bytes_accessed=local_experts * width * both * 2, transcendentals=0
        ),
    )(placed, *parts)


def plus(first, second):
    return first.astype(F32) + second.astype(F32)


def swiglu_grads(gate_act, up_act, hidden_grad):
    sigmoid_gate = jax.nn.sigmoid(gate_act)
    up_grad = (hidden_grad * gate_act * sigmoid_gate).astype(BF16)
    gate_grad = (
        hidden_grad * up_act * sigmoid_gate * (1.0 + gate_act * (1.0 - sigmoid_gate))
    ).astype(BF16)
    return gate_grad, up_grad


def on_small_slice(tokens, cotangent, expert_ids, gate_weight, up_weight, down_weight):
    n_dp, n_x, n_t = 4, 2, 4
    k, x, t = lax.axis_index("dp"), lax.axis_index("expert"), lax.axis_index("tensor")
    width = gate_weight.shape[1]
    rows = tokens.shape[0]
    where = jnp.stack([k, x]).astype(jnp.int32)
    chunks = split(where, expert_ids.reshape(1, rows), tokens, width, n_dp)
    def to_owner(value, rel, flip):
        if rel == 0 and flip == 0:
            return value
        pairs = [
            (i * n_x + j, (i ^ rel) * n_x + (j ^ flip)) for i in range(n_dp) for j in range(n_x)
        ]
        return lax.ppermute(value, ("dp", "expert"), pairs)

    own_tokens = [to_owner(c, rel, 0) for rel, c in enumerate(chunks)]
    near_tokens = [to_owner(c, rel, 1) for rel, c in enumerate(chunks[:2])]
    grads = [lax.dynamic_slice_in_dim(cotangent, (k ^ rel) * width, width, axis=1) for rel in range(n_dp)]
    far_tokens, grads = lax.optimization_barrier((own_tokens[2:], grads))
    near_tokens, far_tokens = lax.optimization_barrier((near_tokens, far_tokens))
    far_tokens = [swap(c, "expert", n_x, 1) for c in far_tokens]
    own_grads = [to_owner(c, rel, 0) for rel, c in enumerate(grads)]
    leaving_grads = jnp.stack(own_grads)
    far_tokens, leaving_grads = lax.optimization_barrier((far_tokens, leaving_grads))
    other_grads = swap(leaving_grads, "expert", n_x, 1)
    gate_weight, up_weight, down_weight = (
        jnp.swapaxes(weight, 1, 2) for weight in (gate_weight, up_weight, down_weight)
    )
    local_experts = gate_weight.shape[0]

    def project(values, weight):
        act = jnp.einsum("esd,ehd->esh", values, weight, preferred_element_type=F32).astype(BF16)
        return jnp.split(act, n_dp, axis=1)

    def near_and_far(act):
        near, far = swap(act[1], "dp", n_dp, 1), swap(act[3], "dp", n_dp, 1)
        return plus(act[0], near), plus(act[2], far).astype(BF16)

    placed, lines = place(where, own_tokens, near_tokens + far_tokens, None, rows, local_experts, [leaving_grads])
    gate_near, gate_far = near_and_far(project(placed, gate_weight))
    up_near, up_far = near_and_far(project(placed, up_weight))
    far = jnp.stack([gate_far, up_far])
    there = swap(far, "dp", n_dp, 2)
    placed_grads = place(where, own_grads, [other_grads], lines, rows, local_experts, [far])
    hidden_act = project(placed_grads, down_weight)
    beside, there = lax.optimization_barrier((swap(hidden_act[3], "dp", n_dp, 1), there))
    hidden_far = plus(hidden_act[2], beside).astype(BF16)
    hidden_near = plus(hidden_act[0], swap(hidden_act[1], "dp", n_dp, 1))
    gate_act, up_act = plus(gate_near, there[0]), plus(up_near, there[1])
    sigmoid_gate = jax.nn.sigmoid(gate_act)
    up_factor = gate_act * sigmoid_gate
    gate_factor = up_act * sigmoid_gate * (1.0 + gate_act * (1.0 - sigmoid_gate))
    hidden_grad = plus(hidden_near, swap(hidden_far, "dp", n_dp, 2))
    part = jnp.concatenate([hidden_grad * gate_factor, hidden_grad * up_factor], axis=2).astype(BF16)
    far = swap(part, "dp", n_dp, 2)
    beside = swap(part, "dp", n_dp, 1)
    near_back = back((0, 1), lines, [part, beside], gate_weight, up_weight, rows)
    far, _ = lax.optimization_barrier((far, near_back[0]))
    parts = [part, beside, far, swap(far, "dp", n_dp, 1)]
    far_back = back((2, 3), lines, parts[2:], gate_weight, up_weight, rows)
    weight_grad = weight_grads(placed, parts, 4)

    def blocks(rels, after, own0, own1, other0, other1):
        owns = [to_owner(own, rel, 0) for rel, own in zip(rels, (own0, own1))]
        others = [to_owner(other, rel, 1) for rel, other in zip(rels, (other0, other1))]
        owns, others, _ = lax.optimization_barrier((owns, others, after))
        terms = [plus(own, other).astype(BF16) for own, other in zip(owns, others)]
        odd = ((k ^ t) & 1) == 1
        keep = jnp.where(odd, terms[1], terms[0])
        leaving = jnp.where(odd, terms[0], terms[1])
        return plus(keep, swap(leaving, "tensor", n_t, 1))

    first, second = blocks((0, 1), far_back[0], *near_back), blocks((2, 3), weight_grad, *far_back)
    swapped = ((k ^ t) & 2) == 2
    keep = jnp.where(swapped, second, first)
    leaving = jnp.where(swapped, first, second).astype(BF16)
    grad_tokens = plus(keep, swap(leaving, "tensor", n_t, 2)).astype(BF16)

    grad_gate, grad_up = (jnp.swapaxes(grad, 1, 2) for grad in weight_grad)
    return grad_tokens, grad_gate, grad_up


def bits_of(count):
    bits = []
    bit = 1
    while bit < count:
        bits.append(bit)
        bit *= 2
    return bits


def halving_sum(parts, axis, count):
    parts = dict(parts)
    for bit in bits_of(count):
        leaving = sorted(r for r in parts if r & bit)
        arrived = swap(jnp.stack([parts[r].astype(BF16) for r in leaving]), axis, count, bit)
        for at, r in enumerate(leaving):
            parts[r ^ bit] = plus(parts[r ^ bit], arrived[at])
            del parts[r]
    return parts[0]


def doubling_gather(value, axis, count):
    held = {0: value}
    for bit in reversed(bits_of(count)):
        known = sorted(held)
        arrived = swap(jnp.stack([held[r] for r in known]), axis, count, bit)
        for at, r in enumerate(known):
            held[r ^ bit] = arrived[at]
    return [held[r] for r in range(count)]


def on_any_slice(tokens, cotangent, expert_ids, gate_weight, up_weight, down_weight):
    n_dp, n_x, n_t = lax.axis_size("dp"), lax.axis_size("expert"), lax.axis_size("tensor")
    k, x, t = lax.axis_index("dp"), lax.axis_index("expert"), lax.axis_index("tensor")
    local_experts, width, hidden = gate_weight.shape
    rows = tokens.shape[0]
    slots = n_x * CAP
    ids_row = expert_ids.reshape(1, rows)
    order = jnp.arange(rows, dtype=jnp.int32)
    earlier = (expert_ids == ids_row) & (order[:, None] < order[None, :])
    position = jnp.sum(earlier.astype(jnp.int32), axis=0)
    target = ids_row[0] * CAP + position
    targets = lax.all_gather(target, ("dp", "expert"), axis=0, tiled=False).reshape(n_dp, n_x, rows)
    pair = jnp.stack([tokens, cotangent])
    placers, slot_rows = [], []
    for rel in range(n_dp):
        columns = lax.dynamic_slice_in_dim(pair, (k ^ rel) * width, width, axis=2)
        mine = columns if rel == 0 else swap(columns, "dp", n_dp, rel)
        blocks = lax.all_gather(mine, "expert", axis=1, tiled=True)
        goal = lax.dynamic_index_in_dim(targets, k ^ rel, axis=0, keepdims=False)
        expert = goal // CAP - x * local_experts
        place = jnp.arange(n_x, dtype=jnp.int32)[:, None] * CAP + goal % CAP
        row = jnp.where((expert >= 0) & (expert < local_experts), expert * slots + place, -1)
        row = row.reshape(1, n_x * rows)
        every = jnp.arange(local_experts * slots, dtype=jnp.int32)[:, None]
        placer = (every == row).astype(BF16)
        placers.append(placer)
        slot_rows.append(
            jnp.einsum("sn,and->asd", placer, blocks, preferred_element_type=F32)
            .astype(BF16)
            .reshape(2, local_experts, slots, width)
        )
    slot_rows = jnp.concatenate(slot_rows, axis=2)
    inputs, grads_in = slot_rows[0], slot_rows[1]

    def act(values, weight):
        return jnp.einsum("esd,edf->esf", values, weight, preferred_element_type=F32).astype(BF16)

    acts = jnp.stack([act(inputs, gate_weight), act(inputs, up_weight), act(grads_in, down_weight)])
    acts = acts.reshape(3, local_experts, n_dp, slots, hidden)
    acts = halving_sum({r: acts[:, :, r] for r in range(n_dp)}, "dp", n_dp)
    grads = doubling_gather(jnp.stack(swiglu_grads(acts[0], acts[1], acts[2])), "dp", n_dp)
    grads = jnp.concatenate(grads, axis=2)
    gate_grad, up_grad = grads[0], grads[1]
    partial_value = jnp.einsum("esf,edf->esd", gate_grad, gate_weight, preferred_element_type=F32)
    partial_value = partial_value + jnp.einsum("esf,edf->esd", up_grad, up_weight, preferred_element_type=F32)
    partial_value = partial_value.astype(BF16).reshape(local_experts, n_dp, slots, width)
    per_token = []
    for rel in range(n_dp):
        flat = partial_value[:, rel].reshape(local_experts * slots, width)
        spread = lax.dot_general(placers[rel], flat, (((0,), (0,)), ((), ())), preferred_element_type=F32)
        spread = spread.astype(BF16).reshape(n_x, rows, width)
        per_token.append(lax.psum_scatter(spread, "expert", scatter_dimension=0, tiled=False))
    per_token = jnp.stack(per_token)
    terms = {r: lax.dynamic_index_in_dim(per_token, k ^ t ^ r, axis=0, keepdims=False) for r in range(n_t)}
    summed = halving_sum(terms, "tensor", n_t).astype(BF16)
    summed = lax.ppermute(
        summed, ("dp", "tensor"), [(i * n_t + j, j * n_t + i) for i in range(n_dp) for j in range(n_t)]
    )
    grad_gate = jnp.einsum("esd,esf->edf", inputs, gate_grad, preferred_element_type=F32).astype(BF16)
    grad_up = jnp.einsum("esd,esf->edf", inputs, up_grad, preferred_element_type=F32).astype(BF16)
    return summed, grad_gate, grad_up


def solution(mesh):
    placed = (
        P(("dp", "expert"), None),
        P(("dp", "expert"), None),
        P(("dp", "expert"), None),
        P("expert", "dp", "tensor"),
        P("expert", "dp", "tensor"),
        P("expert", "dp", "tensor"),
    )
    sizes = tuple(mesh.shape[name] for name in ("dp", "expert", "tensor"))
    return jax.shard_map(
        on_small_slice if sizes == (4, 2, 4) else on_any_slice,
        mesh=mesh,
        in_specs=placed,
        out_specs=(
            P(("dp", "expert"), "tensor"),
            P("expert", "dp", "tensor"),
            P("expert", "dp", "tensor"),
        ),
        check_vma=False,
    )
```

profile of v0, /device:TPU:0, one launch (start us, length us, event | category | flops | bytes accessed | tf_op | source)
XLA Modules:
  0.0 101.6 jit_solution(17733857355009954790)
XLA Ops:
  3.3 3.0 %collective-permute-start.1 = (bf16[144,512]{1,0:T(8,128)(2,1)S(1)}, bf16[144,512]{1,0:T(8,128)(2,1)S(1)}, u32[]{:S(2)}, u32[]{:S(2)}) collective-permute-start(bf16[144,512]{1,0:T(8,128)(2,1)S(1)} %get-tuple-element.45), channel_id=1, source_target_pairs={{0,16},{4,20},{8,24},{12,28},{16,0},{20,4},{24,8},{28,12},{1,17},{... | collective-permute-start | bytes 442376 | tf_op jit(solution)/shard_map/ppermute | solution.py:248
  9.2 1.8 %collective-permute-done.1.refs_2_ = bf16[144,512]{1,0:T(8,128)(2,1)S(1)} collective-permute-done((bf16[144,512]{1,0:T(8,128)(2,1)S(1)}, bf16[144,512]{1,0:T(8,128)(2,1)S(1)}, u32[]{:S(2)}, u32[]{:S(2)}) %collective-permute-start.1) | collective-permute-done | bytes 147488 | tf_op jit(solution)/shard_map/ppermute | solution.py:248
  13.5 1.7 %collective-permute-start.8 = (bf16[128,512]{1,0:T(8,128)(2,1)S(1)}, bf16[128,512]{1,0:T(8,128)(2,1)S(1)}, u32[]{:S(2)}, u32[]{:S(2)}) collective-permute-start(bf16[128,512]{1,0:T(8,128)(2,1)S(1)} %get-tuple-element.55), channel_id=1, source_target_pairs={{0,16},{4,20},{8,24},{12,28},{16,0},{20,4},{24,8},{28,12},{1,17},{... | collective-permute-start | bytes 393224 | tf_op jit(solution)/shard_map/ppermute | solution.py:248
  15.2 1.9 %collective-permute-start.5 = (bf16[144,512]{1,0:T(8,128)(2,1)S(1)}, bf16[144,512]{1,0:T(8,128)(2,1)S(1)}, u32[]{:S(2)}, u32[]{:S(2)}) collective-permute-start(bf16[144,512]{1,0:T(8,128)(2,1)S(1)} %collective-permute-done.1.refs_2_), channel_id=1, source_target_pairs={{0,4},{4,0},{1,5},{5,1},{2,6},{6,2},{3,7},{7,3},{8,12},{12,8},{9,1... | collective-permute-start | bytes 442376 | tf_op jit(solution)/shard_map/ppermute | solution.py:19
  17.3 2.2 %collective-permute-done.8.refs_2_ = bf16[128,512]{1,0:T(8,128)(2,1)S(1)} collective-permute-done((bf16[128,512]{1,0:T(8,128)(2,1)S(1)}, bf16[128,512]{1,0:T(8,128)(2,1)S(1)}, u32[]{:S(2)}, u32[]{:S(2)}) %collective-permute-start.8) | collective-permute-done | bytes 131104 | tf_op jit(solution)/shard_map/ppermute | solution.py:248
  22.0 2.6 %collective-permute-done.6.refs_7_ = bf16[144,512]{1,0:T(8,128)(2,1)S(1)} collective-permute-done((bf16[144,512]{1,0:T(8,128)(2,1)S(1)}, bf16[144,512]{1,0:T(8,128)(2,1)S(1)}, u32[]{:S(2)}, u32[]{:S(2)}) %collective-permute-start.6) | collective-permute-done | bytes 147488 | tf_op jit(solution)/shard_map/ppermute | solution.py:19
  24.5 1.7 %collective-permute-start.10 = (bf16[4,128,512]{2,1,0:T(8,128)(2,1)S(1)}, bf16[4,128,512]{2,1,0:T(8,128)(2,1)S(1)}, u32[]{:S(2)}, u32[]{:S(2)}) collective-permute-start(bf16[4,128,512]{2,1,0:T(8,128)(2,1)S(1)} %pad_maximum_fusion.refs_8_), channel_id=1, source_target_pairs={{0,4},{4,0},{1,5},{5,1},{2,6},{6,2},{3,7},{7,3},{8,12},{12,8},{9,1... | collective-permute-start | bytes 1572872 | tf_op jit(solution)/shard_map/ppermute | solution.py:19
  27.3 1.7 %convolution_convert_fusion.1 = bf16[16,64,352]{2,1,0:T(8,128)(2,1)S(1)} fusion(bf16[16,64,512]{2,1,0:T(8,128)(2,1)S(1)} %get-tuple-element.61.placed, bf16[16,512,352]{1,2,0:T(8,128)(2,1)S(1)} %bitcast.36), kind=kOutput, calls=%fused_computation.1 | convolution fusion | flops 369459200 | bytes 7536640 | tf_op jit(solution)/shard_map/esd,ehd->esh/dot_general | solution.py:266
  29.1 1.7 %convolution_convert_fusion.2 = bf16[16,64,352]{2,1,0:T(8,128)(2,1)S(1)} fusion(bf16[16,64,512]{2,1,0:T(8,128)(2,1)S(1)} %get-tuple-element.61.placed, bf16[16,512,352]{1,2,0:T(8,128)(2,1)S(1)} %bitcast.40), kind=kOutput, calls=%fused_computation.2 | convolution fusion | flops 369459200 | bytes 7536640 | tf_op jit(solution)/shard_map/esd,ehd->esh/dot_general | solution.py:266
  32.6 1.8 %collective-permute-start.15 = (bf16[2,16,16,352]{3,2,1,0:T(8,128)(2,1)S(1)}, bf16[2,16,16,352]{3,2,1,0:T(8,128)(2,1)S(1)}, u32[]{:S(2)}, u32[]{:S(2)}) collective-permute-start(bf16[2,16,16,352]{3,2,1,0:T(8,128)(2,1)S(1)} %pad_maximum_fusion.1.refs_6_), channel_id=1, source_target_pairs={{0,16},{8,24},{16,0},{24,8},{1,17},{9,25},{17,1},{25,9},{2,18},{10... | collective-permute-start | bytes 1081352 | tf_op jit(solution)/shard_map/ppermute | solution.py:19
  34.3 3.5 %collective-permute-done.10.refs_4_ = bf16[4,128,512]{2,1,0:T(8,128)(2,1)S(1)} collective-permute-done((bf16[4,128,512]{2,1,0:T(8,128)(2,1)S(1)}, bf16[4,128,512]{2,1,0:T(8,128)(2,1)S(1)}, u32[]{:S(2)}, u32[]{:S(2)}) %collective-permute-start.10) | collective-permute-done | bytes 524320 | tf_op jit(solution)/shard_map/ppermute | solution.py:19
  42.1 1.9 %collective-permute-done.15 = bf16[2,16,16,352]{3,2,1,0:T(8,128)(2,1)S(1)} collective-permute-done((bf16[2,16,16,352]{3,2,1,0:T(8,128)(2,1)S(1)}, bf16[2,16,16,352]{3,2,1,0:T(8,128)(2,1)S(1)}, u32[]{:S(2)}, u32[]{:S(2)}) %collective-permute-start.15) | collective-permute-done | bytes 360480 | tf_op jit(solution)/shard_map/ppermute | solution.py:19
  44.1 1.8 %collective-permute-start.16 = (bf16[16,16,352]{2,1,0:T(8,128)(2,1)S(1)}, bf16[16,16,352]{2,1,0:T(8,128)(2,1)S(1)}, u32[]{:S(2)}, u32[]{:S(2)}) collective-permute-start(bf16[16,16,352]{2,1,0:T(8,128)(2,1)S(1)} %add_convert_fusion), channel_id=1, source_target_pairs={{0,16},{8,24},{16,0},{24,8},{1,17},{9,25},{17,1},{25,9},{2,18},{10... | collective-permute-start | bytes 540680 | tf_op jit(solution)/shard_map/ppermute | solution.py:19
  45.9 4.7 %collective-permute-done.16 = bf16[16,16,352]{2,1,0:T(8,128)(2,1)S(1)} collective-permute-done((bf16[16,16,352]{2,1,0:T(8,128)(2,1)S(1)}, bf16[16,16,352]{2,1,0:T(8,128)(2,1)S(1)}, u32[]{:S(2)}, u32[]{:S(2)}) %collective-permute-start.16) | collective-permute-done | bytes 180256 | tf_op jit(solution)/shard_map/ppermute | solution.py:19
  51.1 1.8 %collective-permute-start.19 = (bf16[16,16,704]{2,1,0:T(8,128)(2,1)S(1)}, bf16[16,16,704]{2,1,0:T(8,128)(2,1)S(1)}, u32[]{:S(2)}, u32[]{:S(2)}) collective-permute-start(bf16[16,16,704]{2,1,0:T(8,128)(2,1)S(1)} %pad_maximum_fusion.2.h0), channel_id=1, source_target_pairs={{0,16},{8,24},{16,0},{24,8},{1,17},{9,25},{17,1},{25,9},{2,18},{10... | collective-permute-start | bytes 1081352 | tf_op jit(solution)/shard_map/ppermute | solution.py:19
  52.9 5.0 %shard_map.88 = (bf16[128,512]{1,0:T(8,128)(2,1)S(1)}, bf16[128,512]{1,0:T(8,128)(2,1)S(1)}, bf16[128,512]{1,0:T(8,128)(2,1)S(1)}, bf16[128,512]{1,0:T(8,128)(2,1)S(1)}) custom-call(s32[4,8,256]{2,1,0:T(8,128)S(1)} %get-tuple-element.60.refs_5_.lines, bf16[16,16,704]{2,1,0:T(8,128)(2,1)S(1)} %pad_maximum_fusion.2.h0, ...), custom_call_target="tpu_custom_call" | custom-call | flops 1476395008 | bytes 11534336 | tf_op jit(solution)/shard_map/pallas_call | solution.py:174
  57.9 4.7 %collective-permute-done.19.h0.h2 = bf16[16,16,704]{2,1,0:T(8,128)(2,1)S(1)} collective-permute-done((bf16[16,16,704]{2,1,0:T(8,128)(2,1)S(1)}, bf16[16,16,704]{2,1,0:T(8,128)(2,1)S(1)}, u32[]{:S(2)}, u32[]{:S(2)}) %collective-permute-start.19) | collective-permute-done | bytes 360480 | tf_op jit(solution)/shard_map/ppermute | solution.py:19
  64.5 5.0 %shard_map.89 = (bf16[128,512]{1,0:T(8,128)(2,1)S(1)}, bf16[128,512]{1,0:T(8,128)(2,1)S(1)}, bf16[128,512]{1,0:T(8,128)(2,1)S(1)}, bf16[128,512]{1,0:T(8,128)(2,1)S(1)}) custom-call(s32[4,8,256]{2,1,0:T(8,128)S(1)} %get-tuple-element.60.refs_5_.lines, bf16[16,16,704]{2,1,0:T(8,128)(2,1)S(1)} %collective-permute-done.19.h0.h2, ...), custom_call_target="tpu_custom_call" | custom-call | flops 1476395008 | bytes 11534336 | tf_op jit(solution)/shard_map/pallas_call | solution.py:174
  69.6 1.8 %collective-permute-start.22 = (bf16[128,512]{1,0:T(8,128)(2,1)S(1)}, bf16[128,512]{1,0:T(8,128)(2,1)S(1)}, u32[]{:S(2)}, u32[]{:S(2)}) collective-permute-start(bf16[128,512]{1,0:T(8,128)(2,1)S(1)} %get-tuple-element.66), channel_id=1, source_target_pairs={{0,16},{4,20},{8,24},{12,28},{16,0},{20,4},{24,8},{28,12},{1,17},{... | collective-permute-start | bytes 393224 | tf_op jit(solution)/shard_map/ppermute | solution.py:248
  76.8 5.7 %shard_map.90 = (bf16[16,352,512]{2,1,0:T(8,128)(2,1)}, bf16[16,352,512]{2,1,0:T(8,128)(2,1)}) custom-call(bf16[16,64,512]{2,1,0:T(8,128)(2,1)S(1)} %get-tuple-element.61.placed, bf16[16,16,704]{2,1,0:T(8,128)(2,1)S(1)} %pad_maximum_fusion.2.h0, bf16[16,16,704]{2,1,0:T(8,128)(2,1)S(1)} %collective-permute-done.20.h1, ...), custom_call_target="tpu_custom_call" | custom-call | flops 2952790016 | bytes 11534336 | tf_op jit(solution)/shard_map/pallas_call | solution.py:209
  82.5 2.2 %collective-permute-done.23 = bf16[128,512]{1,0:T(8,128)(2,1)S(1)} collective-permute-done((bf16[128,512]{1,0:T(8,128)(2,1)S(1)}, bf16[128,512]{1,0:T(8,128)(2,1)S(1)}, u32[]{:S(2)}, u32[]{:S(2)}) %collective-permute-start.23) | collective-permute-done | bytes 131104 | tf_op jit(solution)/shard_map/ppermute | solution.py:248
  86.5 4.6 %collective-permute-done.26 = bf16[128,512]{1,0:T(8,128)(2,1)S(1)} collective-permute-done((bf16[128,512]{1,0:T(8,128)(2,1)S(1)}, bf16[128,512]{1,0:T(8,128)(2,1)S(1)}, u32[]{:S(2)}, u32[]{:S(2)}) %collective-permute-start.26) | collective-permute-done | bytes 131104 | tf_op jit(solution)/shard_map/ppermute | solution.py:19
  92.4 2.7 %collective-permute-start.31 = (bf16[128,512]{1,0:T(8,128)(2,1)S(1)}, bf16[128,512]{1,0:T(8,128)(2,1)S(1)}, u32[]{:S(2)}, u32[]{:S(2)}) collective-permute-start(bf16[128,512]{1,0:T(8,128)(2,1)S(1)} %get-tuple-element.83), channel_id=1, source_target_pairs={{0,2},{1,3},{2,0},{3,1},{4,6},{5,7},{6,4},{7,5},{8,10},{9,11},{10,... | collective-permute-start | bytes 393224 | tf_op jit(solution)/shard_map/ppermute | solution.py:19
  95.0 5.8 %collective-permute-done.31 = bf16[128,512]{1,0:T(8,128)(2,1)S(1)} collective-permute-done((bf16[128,512]{1,0:T(8,128)(2,1)S(1)}, bf16[128,512]{1,0:T(8,128)(2,1)S(1)}, u32[]{:S(2)}, u32[]{:S(2)}) %collective-permute-start.31) | collective-permute-done | bytes 131104 | tf_op jit(solution)/shard_map/ppermute | solution.py:19
  (90 shorter events, 29.3 us)
Async XLA Ops:
  3.3 7.7 %collective-permute-start.1 = (bf16[144,512]{1,0:T(8,128)(2,1)S(1)}, bf16[144,512]{1,0:T(8,128)(2,1)S(1)}, u32[]{:S(2)}, u32[]{:S(2)}) collective-permute-start(bf16[144,512]{1,0:T(8,128)(2,1)S(1)} %get-tuple-element.45), channel_id=1, source_target_pairs={{0,16},{4,20},{8,24},{12,28},{16,0},{20,4},{24,8},{28,12},{1,17},{... | collective-permute-start | bytes 442376 | tf_op jit(solution)/shard_map/ppermute | solution.py:248
  6.3 6.3 %collective-permute-start.2 = (bf16[144,512]{1,0:T(8,128)(2,1)S(1)}, bf16[144,512]{1,0:T(8,128)(2,1)S(1)}, u32[]{:S(2)}, u32[]{:S(2)}) collective-permute-start(bf16[144,512]{1,0:T(8,128)(2,1)S(1)} %get-tuple-element.46), channel_id=1, source_target_pairs={{0,24},{4,28},{8,16},{12,20},{16,8},{20,12},{24,0},{28,4},{1,25},{... | collective-permute-start | bytes 442376 | tf_op jit(solution)/shard_map/ppermute | solution.py:248
  6.3 8.9 %collective-permute-start.3 = (bf16[144,512]{1,0:T(8,128)(2,1)S(1)}, bf16[144,512]{1,0:T(8,128)(2,1)S(1)}, u32[]{:S(2)}, u32[]{:S(2)}) collective-permute-start(bf16[144,512]{1,0:T(8,128)(2,1)S(1)} %get-tuple-element.43.refs_0_), channel_id=1, source_target_pairs={{0,4},{4,0},{8,12},{12,8},{16,20},{20,16},{24,28},{28,24},{1,5},{5... | collective-permute-start | bytes 442376 | tf_op jit(solution)/shard_map/ppermute | solution.py:248
  7.8 7.4 %collective-permute-start.4 = (bf16[144,512]{1,0:T(8,128)(2,1)S(1)}, bf16[144,512]{1,0:T(8,128)(2,1)S(1)}, u32[]{:S(2)}, u32[]{:S(2)}) collective-permute-start(bf16[144,512]{1,0:T(8,128)(2,1)S(1)} %get-tuple-element.44), channel_id=1, source_target_pairs={{0,12},{4,8},{8,4},{12,0},{16,28},{20,24},{24,20},{28,16},{1,13},{... | collective-permute-start | bytes 442376 | tf_op jit(solution)/shard_map/ppermute | solution.py:248
  13.5 6.1 %collective-permute-start.8 = (bf16[128,512]{1,0:T(8,128)(2,1)S(1)}, bf16[128,512]{1,0:T(8,128)(2,1)S(1)}, u32[]{:S(2)}, u32[]{:S(2)}) collective-permute-start(bf16[128,512]{1,0:T(8,128)(2,1)S(1)} %get-tuple-element.55), channel_id=1, source_target_pairs={{0,16},{4,20},{8,24},{12,28},{16,0},{20,4},{24,8},{28,12},{1,17},{... | collective-permute-start | bytes 393224 | tf_op jit(solution)/shard_map/ppermute | solution.py:248
  15.2 5.8 %collective-permute-start.9 = (bf16[128,512]{1,0:T(8,128)(2,1)S(1)}, bf16[128,512]{1,0:T(8,128)(2,1)S(1)}, u32[]{:S(2)}, u32[]{:S(2)}) collective-permute-start(bf16[128,512]{1,0:T(8,128)(2,1)S(1)} %get-tuple-element.56), channel_id=1, source_target_pairs={{0,24},{4,28},{8,16},{12,20},{16,8},{20,12},{24,0},{28,4},{1,25},{... | collective-permute-start | bytes 393224 | tf_op jit(solution)/shard_map/ppermute | solution.py:248
  15.2 6.7 %collective-permute-start.5 = (bf16[144,512]{1,0:T(8,128)(2,1)S(1)}, bf16[144,512]{1,0:T(8,128)(2,1)S(1)}, u32[]{:S(2)}, u32[]{:S(2)}) collective-permute-start(bf16[144,512]{1,0:T(8,128)(2,1)S(1)} %collective-permute-done.1.refs_2_), channel_id=1, source_target_pairs={{0,4},{4,0},{1,5},{5,1},{2,6},{6,2},{3,7},{7,3},{8,12},{12,8},{9,1... | collective-permute-start | bytes 442376 | tf_op jit(solution)/shard_map/ppermute | solution.py:19
  17.1 7.4 %collective-permute-start.6 = (bf16[144,512]{1,0:T(8,128)(2,1)S(1)}, bf16[144,512]{1,0:T(8,128)(2,1)S(1)}, u32[]{:S(2)}, u32[]{:S(2)}) collective-permute-start(bf16[144,512]{1,0:T(8,128)(2,1)S(1)} %collective-permute-done.2.refs_3_), channel_id=1, source_target_pairs={{0,4},{4,0},{1,5},{5,1},{2,6},{6,2},{3,7},{7,3},{8,12},{12,8},{9,1... | collective-permute-start | bytes 442376 | tf_op jit(solution)/shard_map/ppermute | solution.py:19
  17.3 8.9 %collective-permute-start = (bf16[144,512]{1,0:T(8,128)(2,1)S(1)}, bf16[144,512]{1,0:T(8,128)(2,1)S(1)}, u32[]{:S(2)}, u32[]{:S(2)}) collective-permute-start(bf16[144,512]{1,0:T(8,128)(2,1)S(1)} %get-tuple-element.44), channel_id=1, source_target_pairs={{0,8},{4,12},{8,0},{12,4},{16,24},{20,28},{24,16},{28,20},{1,9},{5... | collective-permute-start | bytes 442376 | tf_op jit(solution)/shard_map/ppermute | solution.py:248
  24.5 13.4 %collective-permute-start.10 = (bf16[4,128,512]{2,1,0:T(8,128)(2,1)S(1)}, bf16[4,128,512]{2,1,0:T(8,128)(2,1)S(1)}, u32[]{:S(2)}, u32[]{:S(2)}) collective-permute-start(bf16[4,128,512]{2,1,0:T(8,128)(2,1)S(1)} %pad_maximum_fusion.refs_8_), channel_id=1, source_target_pairs={{0,4},{4,0},{1,5},{5,1},{2,6},{6,2},{3,7},{7,3},{8,12},{12,8},{9,1... | collective-permute-start | bytes 1572872 | tf_op jit(solution)/shard_map/ppermute | solution.py:19
  32.6 11.5 %collective-permute-start.15 = (bf16[2,16,16,352]{3,2,1,0:T(8,128)(2,1)S(1)}, bf16[2,16,16,352]{3,2,1,0:T(8,128)(2,1)S(1)}, u32[]{:S(2)}, u32[]{:S(2)}) collective-permute-start(bf16[2,16,16,352]{3,2,1,0:T(8,128)(2,1)S(1)} %pad_maximum_fusion.1.refs_6_), channel_id=1, source_target_pairs={{0,16},{8,24},{16,0},{24,8},{1,17},{9,25},{17,1},{25,9},{2,18},{10... | collective-permute-start | bytes 1081352 | tf_op jit(solution)/shard_map/ppermute | solution.py:19
  41.1 4.8 %collective-permute-start.17 = (bf16[16,16,352]{2,1,0:T(8,128)(2,1)S(1)}, bf16[16,16,352]{2,1,0:T(8,128)(2,1)S(1)}, u32[]{:S(2)}, u32[]{:S(2)}) collective-permute-start(bf16[16,16,352]{2,1,0:T(8,128)(2,1)S(1)} %get-tuple-element.88), channel_id=1, source_target_pairs={{0,8},{8,0},{16,24},{24,16},{1,9},{9,1},{17,25},{25,17},{2,10},{10... | collective-permute-start | bytes 540680 | tf_op jit(solution)/shard_map/ppermute | solution.py:19
  44.1 6.4 %collective-permute-start.16 = (bf16[16,16,352]{2,1,0:T(8,128)(2,1)S(1)}, bf16[16,16,352]{2,1,0:T(8,128)(2,1)S(1)}, u32[]{:S(2)}, u32[]{:S(2)}) collective-permute-start(bf16[16,16,352]{2,1,0:T(8,128)(2,1)S(1)} %add_convert_fusion), channel_id=1, source_target_pairs={{0,16},{8,24},{16,0},{24,8},{1,17},{9,25},{17,1},{25,9},{2,18},{10... | collective-permute-start | bytes 540680 | tf_op jit(solution)/shard_map/ppermute | solution.py:19
  51.1 11.5 %collective-permute-start.19 = (bf16[16,16,704]{2,1,0:T(8,128)(2,1)S(1)}, bf16[16,16,704]{2,1,0:T(8,128)(2,1)S(1)}, u32[]{:S(2)}, u32[]{:S(2)}) collective-permute-start(bf16[16,16,704]{2,1,0:T(8,128)(2,1)S(1)} %pad_maximum_fusion.2.h0), channel_id=1, source_target_pairs={{0,16},{8,24},{16,0},{24,8},{1,17},{9,25},{17,1},{25,9},{2,18},{10... | collective-permute-start | bytes 1081352 | tf_op jit(solution)/shard_map/ppermute | solution.py:19
  62.7 8.7 %collective-permute-start.27 = (bf16[128,512]{1,0:T(8,128)(2,1)S(1)}, bf16[128,512]{1,0:T(8,128)(2,1)S(1)}, u32[]{:S(2)}, u32[]{:S(2)}) collective-permute-start(bf16[128,512]{1,0:T(8,128)(2,1)S(1)} %get-tuple-element.76), channel_id=1, source_target_pairs={{0,8},{4,12},{8,0},{12,4},{16,24},{20,28},{24,16},{28,20},{1,9},{5... | collective-permute-start | bytes 393224 | tf_op jit(solution)/shard_map/ppermute | solution.py:248
  63.2 8.2 %collective-permute-start.28 = (bf16[128,512]{1,0:T(8,128)(2,1)S(1)}, bf16[128,512]{1,0:T(8,128)(2,1)S(1)}, u32[]{:S(2)}, u32[]{:S(2)}) collective-permute-start(bf16[128,512]{1,0:T(8,128)(2,1)S(1)} %get-tuple-element.77), channel_id=1, source_target_pairs={{0,4},{4,0},{8,12},{12,8},{16,20},{20,16},{24,28},{28,24},{1,5},{5... | collective-permute-start | bytes 393224 | tf_op jit(solution)/shard_map/ppermute | solution.py:248
  63.8 7.5 %collective-permute-start.29 = (bf16[128,512]{1,0:T(8,128)(2,1)S(1)}, bf16[128,512]{1,0:T(8,128)(2,1)S(1)}, u32[]{:S(2)}, u32[]{:S(2)}) collective-permute-start(bf16[128,512]{1,0:T(8,128)(2,1)S(1)} %get-tuple-element.78), channel_id=1, source_target_pairs={{0,12},{4,8},{8,4},{12,0},{16,28},{20,24},{24,20},{28,16},{1,13},{... | collective-permute-start | bytes 393224 | tf_op jit(solution)/shard_map/ppermute | solution.py:248
  69.6 15.2 %collective-permute-start.22 = (bf16[128,512]{1,0:T(8,128)(2,1)S(1)}, bf16[128,512]{1,0:T(8,128)(2,1)S(1)}, u32[]{:S(2)}, u32[]{:S(2)}) collective-permute-start(bf16[128,512]{1,0:T(8,128)(2,1)S(1)} %get-tuple-element.66), channel_id=1, source_target_pairs={{0,16},{4,20},{8,24},{12,28},{16,0},{20,4},{24,8},{28,12},{1,17},{... | collective-permute-start | bytes 393224 | tf_op jit(solution)/shard_map/ppermute | solution.py:248
  72.1 14.5 %collective-permute-start.30 = (bf16[128,512]{1,0:T(8,128)(2,1)}, bf16[128,512]{1,0:T(8,128)(2,1)S(1)}, u32[]{:S(2)}, u32[]{:S(2)}) collective-permute-start(bf16[128,512]{1,0:T(8,128)(2,1)} %broadcast_select_fusion), channel_id=1, source_target_pairs={{0,1},{1,0},{2,3},{3,2},{4,5},{5,4},{6,7},{7,6},{8,9},{9,8},{10,11... | collective-permute-start | bytes 393224 | tf_op jit(solution)/shard_map/ppermute | solution.py:19
  73.7 11.1 %collective-permute-start.23 = (bf16[128,512]{1,0:T(8,128)(2,1)S(1)}, bf16[128,512]{1,0:T(8,128)(2,1)S(1)}, u32[]{:S(2)}, u32[]{:S(2)}) collective-permute-start(bf16[128,512]{1,0:T(8,128)(2,1)S(1)} %get-tuple-element.67), channel_id=1, source_target_pairs={{0,24},{4,28},{8,16},{12,20},{16,8},{20,12},{24,0},{28,4},{1,25},{... | collective-permute-start | bytes 393224 | tf_op jit(solution)/shard_map/ppermute | solution.py:248
  74.5 10.2 %collective-permute-start.24 = (bf16[128,512]{1,0:T(8,128)(2,1)S(1)}, bf16[128,512]{1,0:T(8,128)(2,1)S(1)}, u32[]{:S(2)}, u32[]{:S(2)}) collective-permute-start(bf16[128,512]{1,0:T(8,128)(2,1)S(1)} %get-tuple-element.68), channel_id=1, source_target_pairs={{0,20},{4,16},{8,28},{12,24},{16,4},{20,0},{24,12},{28,8},{1,21},{... | collective-permute-start | bytes 393224 | tf_op jit(solution)/shard_map/ppermute | solution.py:248
  75.5 9.3 %collective-permute-start.25 = (bf16[128,512]{1,0:T(8,128)(2,1)S(1)}, bf16[128,512]{1,0:T(8,128)(2,1)S(1)}, u32[]{:S(2)}, u32[]{:S(2)}) collective-permute-start(bf16[128,512]{1,0:T(8,128)(2,1)S(1)} %get-tuple-element.69), channel_id=1, source_target_pairs={{0,28},{4,24},{8,20},{12,16},{16,12},{20,8},{24,4},{28,0},{1,29},{... | collective-permute-start | bytes 393224 | tf_op jit(solution)/shard_map/ppermute | solution.py:248
  85.5 5.6 %collective-permute-start.26 = (bf16[128,512]{1,0:T(8,128)(2,1)S(1)}, bf16[128,512]{1,0:T(8,128)(2,1)S(1)}, u32[]{:S(2)}, u32[]{:S(2)}) collective-permute-start(bf16[128,512]{1,0:T(8,128)(2,1)S(1)} %broadcast_select_fusion.2), channel_id=1, source_target_pairs={{0,1},{1,0},{2,3},{3,2},{4,5},{5,4},{6,7},{7,6},{8,9},{9,8},{10,11... | collective-permute-start | bytes 393224 | tf_op jit(solution)/shard_map/ppermute | solution.py:19
  92.4 8.5 %collective-permute-start.31 = (bf16[128,512]{1,0:T(8,128)(2,1)S(1)}, bf16[128,512]{1,0:T(8,128)(2,1)S(1)}, u32[]{:S(2)}, u32[]{:S(2)}) collective-permute-start(bf16[128,512]{1,0:T(8,128)(2,1)S(1)} %get-tuple-element.83), channel_id=1, source_target_pairs={{0,2},{1,3},{2,0},{3,1},{4,6},{5,7},{6,4},{7,5},{8,10},{9,11},{10,... | collective-permute-start | bytes 393224 | tf_op jit(solution)/shard_map/ppermute | solution.py:19
  (19 other events, 75.5 us)
where the time goes:
time: 102 us
  waiting for transfers between devices  39.1 us (38%)
  starting transfers between devices  30.2 us (30%)
  Pallas kernels  18.7 us (18%)
  matrix products  5 us (5%)
  local copies, waits for them, and re-layouts  4.09 us (4%)
  other arithmetic  3.65 us (4%)
    ppermute x17, waiting for transfers between devices, swap(): return lax.ppermute(value, axis, [(i, i ^ bit) for i in range(count)])  29.7 us
    ppermute x17, starting transfers between devices, swap(): return lax.ppermute(value, axis, [(i, i ^ bit) for i in range(count)])  16.1 us
    ppermute x15, starting transfers between devices, to_owner(): return lax.ppermute(value, ('dp', 'expert'), pairs)  14.1 us
    pallas_call x2, Pallas kernels, back(): pl.pallas_call(functools.partial(back_kernel, rels), out_shape=[jax.Shape...  10.1 us
    ppermute x15, waiting for transfers between devices, to_owner(): return lax.ppermute(value, ('dp', 'expert'), pairs)  9.33 us
    pallas_call x1, Pallas kernels, weight_grads(): pl.pallas_call(weight_kernel, grid=(local_experts // per_step,), out_shap...  5.74 us
    dot_general x3, matrix products, project(): jnp.einsum('esd,ehd->esh', values, weight, preferred_element_type=F32)  5 us
    unnamed x22, local copies, waits for them, and re-layouts  2.83 us
  transfers between devices with their start and end apart: 32, of which 14 were waited for; matrix products, arithmetic and copies ran while one was open for 7% of the time, Pallas kernels for 18%

commit v1 on v0

--- a/solution.py
+++ b/solution.py
@@ -25,53 +25,6 @@
 
 def params(mib=16):
     return pltpu.CompilerParams(vmem_limit_bytes=mib * MIB)
-
-
-def split_kernel(width, n_dp, where, ids, tokens, *refs):
-    outs, (meta, sems) = refs[:-2], refs[-2:]
-    k, x = where[0], where[1]
-    rows = tokens.shape[0]
-    copies = []
-    for rel in range(n_dp):
-        start = pl.multiple_of((k ^ rel) * width, 128)
-        copy = pltpu.make_async_copy(
-            tokens.at[:, pl.ds(start, width)], outs[rel].at[pl.ds(0, rows), :], sems.at[rel]
-        )
-        copy.start()
-        copies.append(copy)
-    along = ids[...].astype(F32)
-    line = lax.broadcasted_iota(jnp.int32, (rows, rows), 0)
-    lane = lax.broadcasted_iota(jnp.int32, (rows, rows), 1)
-    named = jnp.broadcast_to(along, (rows, rows))
-    down = jnp.sum(jnp.where(line == lane, named, 0.0), axis=1, keepdims=True)
-    earlier = jnp.where((named == down) & (line < lane), 1.0, 0.0)
-    place = jnp.sum(earlier, axis=0, keepdims=True) + (x * CAP).astype(F32)
-    at = lax.broadcasted_iota(jnp.int32, (META, rows), 0)
-    meta[...] = jnp.zeros(meta.shape, BF16)
-    meta[:, 0:rows] = jnp.where(at == 0, along, jnp.where(at == 1, place, 0.0)).astype(BF16)
-    for rel in range(n_dp):
-        copy = pltpu.make_async_copy(meta, outs[rel].at[pl.ds(rows, META), :], sems.at[n_dp + rel])
-        copy.start()
-        copies.append(copy)
-    for copy in copies:
-        copy.wait()
-
-
-def split(where, ids, tokens, width, n_dp):
-    rows = tokens.shape[0]
-    anywhere = pl.BlockSpec(memory_space=pl.ANY)
-    return pl.pallas_call(
-        functools.partial(split_kernel, width, n_dp),
-        out_shape=[jax.ShapeDtypeStruct((rows + META, width), BF16)] * n_dp,
-        in_specs=[
-            pl.BlockSpec(memory_space=pltpu.SMEM),
-            pl.BlockSpec(memory_space=pltpu.VMEM),
-            anywhere,
-        ],
-        out_specs=[anywhere] * n_dp,
-        scratch_shapes=[pltpu.VMEM((META, width), BF16), pltpu.SemaphoreType.DMA((2 * n_dp,))],
-        compiler_params=params(),
-    )(where, ids, tokens)
 
 
 def placer_of(row, slot_count):
@@ -133,16 +86,22 @@
     )(where, *mine, *operands, *after)
 
 
-def back_kernel(rels, lines, h0, h1, gate, up, own0, own1, other0, other1, near, held, sems):
+def back_kernel(rels, first, last, *refs):
+    if first:
+        earlier, refs = refs[0], refs[1:]
+    if last:
+        lines, refs = refs[0], refs[1:]
+    h0, h1, gate, up = refs[:4]
+    outs, near, sems = refs[4:-2], refs[-2], refs[-1]
     parts = (h0, h1)
-    local_experts, slots, _ = h0.shape
+    count, slots, _ = h0.shape
     hidden = gate.shape[1]
-    per_copy = local_experts // sems.shape[1]
+    per_copy = count // sems.shape[1]
 
     def copy_of(which, at):
-        group = pl.ds(at * per_copy, per_copy)
         rows = pl.ds(which * hidden, hidden)
-        return pltpu.make_async_copy((gate, up)[which].at[group], near.at[group, rows], sems.at[which, at])
+        source = (gate, up)[which].at[pl.ds(first + at * per_copy, per_copy)]
+        return pltpu.make_async_copy(source, near.at[pl.ds(at * per_copy, per_copy), rows], sems.at[which, at])
 
     for at in range(sems.shape[1]):
         for which in range(2):
@@ -154,8 +113,16 @@
             grads = jnp.concatenate([h[e] for h in parts], axis=0)
             value = jnp.dot(grads, near[e], preferred_element_type=F32).astype(BF16)
             for i in range(2):
-                held[i, e * slots : (e + 1) * slots, :] = value[i * slots : (i + 1) * slots]
-
+                rows = value[i * slots : (i + 1) * slots]
+                if last:
+                    outs[-1][i, (first + e) * slots : (first + e + 1) * slots, :] = rows
+                else:
+                    outs[0][i, e * slots : (e + 1) * slots, :] = rows
+    if not last:
+        return
+    own0, own1, other0, other1, held = outs
+    if first:
+        held[:, 0 : first * slots, :] = earlier[...]
     rows = own0.shape[0]
     for i, (own, other) in enumerate(((own0, other0), (own1, other1))):
         placer = placer_of(lines[rels[i]][0:1], held.shape[1])
@@ -166,26 +133,33 @@
         other[...] = token_rows[rows:]
 
 
-def back(rels, lines, parts, gate, up, rows):
+def back(rels, lines, parts, gate, up, rows, first=0, earlier=None):
     local_experts, hidden, width = gate.shape
-    slots = parts[0].shape[1]
+    count, slots, _ = parts[0].shape
+    last = first + count == local_experts
     vmem = pl.BlockSpec(memory_space=pltpu.VMEM)
-    flops = 4 * local_experts * 2 * slots * width * hidden
+    flops = (16 if last else 1) * count * 2 * slots * width * hidden
+    operands = ([earlier] if first else []) + ([lines] if last else []) + [*parts]
+    near = [
+        pltpu.VMEM((count, 2 * hidden, width), BF16),
+        pltpu.SemaphoreType.DMA((2, count // 2 if count % 2 == 0 else count)),
+    ]
+    if last:
+        out_shape = [jax.ShapeDtypeStruct((rows, width), BF16)] * 4
+        near = [pltpu.VMEM((2, local_experts * slots, width), BF16)] + near
+    else:
+        out_shape = jax.ShapeDtypeStruct((2, count * slots, width), BF16)
     return pl.pallas_call(
-        functools.partial(back_kernel, rels),
-        out_shape=[jax.ShapeDtypeStruct((rows, width), BF16)] * 4,
-        in_specs=[vmem] * 3 + [pl.BlockSpec(memory_space=pl.ANY)] * 2,
-        out_specs=[vmem] * 4,
-        scratch_shapes=[
-            pltpu.VMEM((local_experts, 2 * hidden, width), BF16),
-            pltpu.VMEM((2, local_experts * slots, width), BF16),
-            pltpu.SemaphoreType.DMA((2, 8 if local_experts % 8 == 0 else 1)),
-        ],
+        functools.partial(back_kernel, rels, first, last),
+        out_shape=out_shape,
+        in_specs=[vmem] * len(operands) + [pl.BlockSpec(memory_space=pltpu.HBM)] * 2,
+        out_specs=[vmem] * 4 if last else vmem,
+        scratch_shapes=near,
         compiler_params=params(48),
         cost_estimate=pl.CostEstimate(
-            flops=4 * flops, bytes_accessed=2 * local_experts * width * hidden * 2, transcendentals=0
+            flops=flops, bytes_accessed=2 * count * width * hidden * 2 if last else width, transcendentals=0
         ),
-    )(lines, *parts, gate, up)
+    )(*operands, gate, up)
 
 
 def weight_kernel(placed, h0, h1, h2, h3, gate, up):
@@ -212,7 +186,7 @@
         out_shape=[jax.ShapeDtypeStruct((local_experts, hidden, width), BF16)] * 2,
         in_specs=[pl.BlockSpec((per_step, slot_rows, width), lambda e: (e, 0, 0))] + [part_spec] * len(parts),
         out_specs=[out_spec] * 2,
-        compiler_params=params(24),
+        compiler_params=params(12),
         cost_estimate=pl.CostEstimate(
             flops=4 * flops, bytes_accessed=local_experts * width * both * 2, transcendentals=0
         ),
@@ -238,7 +212,18 @@
     width = gate_weight.shape[1]
     rows = tokens.shape[0]
     where = jnp.stack([k, x]).astype(jnp.int32)
-    chunks = split(where, expert_ids.reshape(1, rows), tokens, width, n_dp)
+    ids_row = expert_ids.reshape(1, rows)
+    order = jnp.arange(rows, dtype=jnp.int32)
+    earlier = (expert_ids == ids_row) & (order[:, None] < order[None, :])
+    position = jnp.sum(earlier.astype(jnp.int32), axis=0, keepdims=True) + x * CAP
+    meta = jnp.concatenate([ids_row, position], axis=0).astype(BF16)
+    meta = jnp.pad(meta, ((0, META - 2), (0, width - rows)))
+
+    def columns(values, rel):
+        return lax.dynamic_slice_in_dim(values, (k ^ rel) * width, width, axis=1)
+
+    chunks = [jnp.concatenate([columns(tokens, rel), meta], axis=0) for rel in range(n_dp)]
+
     def to_owner(value, rel, flip):
         if rel == 0 and flip == 0:
             return value
@@ -249,7 +234,7 @@
 
     own_tokens = [to_owner(c, rel, 0) for rel, c in enumerate(chunks)]
     near_tokens = [to_owner(c, rel, 1) for rel, c in enumerate(chunks[:2])]
-    grads = [lax.dynamic_slice_in_dim(cotangent, (k ^ rel) * width, width, axis=1) for rel in range(n_dp)]
+    grads = [columns(cotangent, rel) for rel in range(n_dp)]
     far_tokens, grads = lax.optimization_barrier((own_tokens[2:], grads))
     near_tokens, far_tokens = lax.optimization_barrier((near_tokens, far_tokens))
     far_tokens = [swap(c, "expert", n_x, 1) for c in far_tokens]
@@ -286,13 +271,19 @@
     gate_factor = up_act * sigmoid_gate * (1.0 + gate_act * (1.0 - sigmoid_gate))
     hidden_grad = plus(hidden_near, swap(hidden_far, "dp", n_dp, 2))
     part = jnp.concatenate([hidden_grad * gate_factor, hidden_grad * up_factor], axis=2).astype(BF16)
-    far = swap(part, "dp", n_dp, 2)
+    count = local_experts * 3 // 8
+    far = [swap(piece, "dp", n_dp, 2) for piece in jnp.split(part, [count], axis=0)]
     beside = swap(part, "dp", n_dp, 1)
     near_back = back((0, 1), lines, [part, beside], gate_weight, up_weight, rows)
-    far, _ = lax.optimization_barrier((far, near_back[0]))
-    parts = [part, beside, far, swap(far, "dp", n_dp, 1)]
-    far_back = back((2, 3), lines, parts[2:], gate_weight, up_weight, rows)
-    weight_grad = weight_grads(placed, parts, 4)
+    far[0], _ = lax.optimization_barrier((far[0], near_back[0]))
+    far_beside = [swap(far[0], "dp", n_dp, 1)]
+    early = back((2, 3), lines, [far[0], far_beside[0]], gate_weight, up_weight, rows)
+    far[1], _ = lax.optimization_barrier((far[1], early))
+    far_beside.append(swap(far[1], "dp", n_dp, 1))
+    far_back = back((2, 3), lines, [far[1], far_beside[1]], gate_weight, up_weight, rows, count, early)
+    parts = [part, beside, jnp.concatenate(far, axis=0), jnp.concatenate(far_beside, axis=0)]
+    after_back, _ = lax.optimization_barrier((placed, far_back[0]))
+    weight_grad = weight_grads(after_back, parts, 4)
 
     def blocks(rels, after, own0, own1, other0, other1):
         owns = [to_owner(own, rel, 0) for rel, own in zip(rels, (own0, own1))]

time: 102 us -> 100 us (0.980)
  waiting for transfers between devices: 39.1 us -> 36.4 us
  starting transfers between devices: 30.2 us -> 31.6 us
  local copies, waits for them, and re-layouts: 4.09 us -> 2.86 us
    ppermute x17 -> x19, waiting for transfers between devices: 29.7 us -> 26.6 us  [swap(): return lax.ppermute(value, axis, [(i, i ^ bit) for i in range(count)])]
    unnamed x22 -> x20, local copies, waits for them, and re-layouts: 2.83 us -> 0.46 us
    dynamic_slice x1 -> x2, local copies, waits for them, and re-layouts: 1.13 us -> 2.28 us  [columns(): return lax.dynamic_slice_in_dim(values, (k ^ rel) * width, width, axis=1)]
    convert_element_type x1, other arithmetic: 1.21 us -> 0.18 us  [on_small_slice(): leaving = jnp.where(swapped, first, second).astype(BF16)]
    ppermute x17 -> x19, starting transfers between devices: 16.1 us -> 17 us  [swap(): return lax.ppermute(value, axis, [(i, i ^ bit) for i in range(count)])]
  transfers between devices with their start and end apart: 32 -> 34, of which waited for: 14 -> 16; matrix products, arithmetic and copies ran while one was open for 7% -> 7% of each run, Pallas kernels for 18% -> 19%
where the time goes in v1:
time: 100 us; the launch traced here: 99.8 us
  waiting for transfers between devices  36.4 us (36%)
  starting transfers between devices  31.6 us (32%)
  Pallas kernels  19.2 us (19%)
  matrix products  4.96 us (5%)
  other arithmetic  3.82 us (4%)
  local copies, waits for them, and re-layouts  2.86 us (3%)
  between operations  1.02 us (1%)
    ppermute x19, waiting for transfers between devices, swap(): return lax.ppermute(value, axis, [(i, i ^ bit) for i in range(count)])  26.6 us
    ppermute x19, starting transfers between devices, swap(): return lax.ppermute(value, axis, [(i, i ^ bit) for i in range(count)])  17 us
    ppermute x15, starting transfers between devices, to_owner(): return lax.ppermute(value, ('dp', 'expert'), pairs)  14.5 us
    pallas_call x3, Pallas kernels, back(): pl.pallas_call(functools.partial(back_kernel, rels, first, last), out_sha...  11.4 us
    ppermute x15, waiting for transfers between devices, to_owner(): return lax.ppermute(value, ('dp', 'expert'), pairs)  9.83 us
    pallas_call x1, Pallas kernels, weight_grads(): pl.pallas_call(weight_kernel, grid=(local_experts // per_step,), out_shap...  5.78 us
    dot_general x3, matrix products, project(): jnp.einsum('esd,ehd->esh', values, weight, preferred_element_type=F32)  4.96 us
    dynamic_slice x2, local copies, waits for them, and re-layouts, columns(): return lax.dynamic_slice_in_dim(values, (k ^ rel) * width, width, axis=1)  2.28 us
  transfers between devices with their start and end apart: 34, of which 16 were waited for; matrix products, arithmetic and copies ran while one was open for 7% of the time, Pallas kernels for 19%

profile of v1, /device:TPU:0, one launch (start us, length us, event | category | flops | bytes accessed | tf_op | source)
XLA Modules:
  0.0 99.8 jit_solution(13241695912112081658)
XLA Ops:
  3.4 2.5 %collective-permute-start.1 = (bf16[144,512]{1,0:T(8,128)(2,1)S(1)}, bf16[144,512]{1,0:T(8,128)(2,1)S(1)}, u32[]{:S(2)}, u32[]{:S(2)}) collective-permute-start(bf16[144,512]{1,0:T(8,128)(2,1)S(1)} %get-tuple-element.98), channel_id=1, source_target_pairs={{0,24},{4,28},{8,16},{12,20},{16,8},{20,12},{24,0},{28,4},{1,25},{... | collective-permute-start | bytes 442376 | tf_op jit(solution)/shard_map/ppermute | solution.py:233
  10.1 3.3 %collective-permute-done.refs_2_ = bf16[144,512]{1,0:T(8,128)(2,1)S(1)} collective-permute-done((bf16[144,512]{1,0:T(8,128)(2,1)S(1)}, bf16[144,512]{1,0:T(8,128)(2,1)S(1)}, u32[]{:S(2)}, u32[]{:S(2)}) %collective-permute-start) | collective-permute-done | bytes 147488 | tf_op jit(solution)/shard_map/ppermute | solution.py:233
  13.4 2.4 %collective-permute-start.3 = (bf16[128,512]{1,0:T(8,128)(2,1)S(1)}, bf16[128,512]{1,0:T(8,128)(2,1)S(1)}, u32[]{:S(2)}, u32[]{:S(2)}) collective-permute-start(bf16[128,512]{1,0:T(8,128)(2,1)S(1)} %get-tuple-element.43), channel_id=1, source_target_pairs={{0,16},{4,20},{8,24},{12,28},{16,0},{20,4},{24,8},{28,12},{1,17},{... | collective-permute-start | bytes 393224 | tf_op jit(solution)/shard_map/ppermute | solution.py:233
  16.0 1.9 %collective-permute-start.7 = (bf16[144,512]{1,0:T(8,128)(2,1)S(1)}, bf16[144,512]{1,0:T(8,128)(2,1)S(1)}, u32[]{:S(2)}, u32[]{:S(2)}) collective-permute-start(bf16[144,512]{1,0:T(8,128)(2,1)S(1)} %collective-permute-done.refs_2_), channel_id=1, source_target_pairs={{0,4},{4,0},{1,5},{5,1},{2,6},{6,2},{3,7},{7,3},{8,12},{12,8},{9,1... | collective-permute-start | bytes 442376 | tf_op jit(solution)/shard_map/ppermute | solution.py:19
  18.1 2.1 %collective-permute-done.3.refs_2_ = bf16[128,512]{1,0:T(8,128)(2,1)S(1)} collective-permute-done((bf16[128,512]{1,0:T(8,128)(2,1)S(1)}, bf16[128,512]{1,0:T(8,128)(2,1)S(1)}, u32[]{:S(2)}, u32[]{:S(2)}) %collective-permute-start.3) | collective-permute-done | bytes 131104 | tf_op jit(solution)/shard_map/ppermute | solution.py:233
  20.2 2.3 %collective-permute-done.4.refs_3_ = bf16[128,512]{1,0:T(8,128)(2,1)S(1)} collective-permute-done((bf16[128,512]{1,0:T(8,128)(2,1)S(1)}, bf16[128,512]{1,0:T(8,128)(2,1)S(1)}, u32[]{:S(2)}, u32[]{:S(2)}) %collective-permute-start.4) | collective-permute-done | bytes 131104 | tf_op jit(solution)/shard_map/ppermute | solution.py:233
  22.7 2.7 %collective-permute-done.8.refs_7_ = bf16[144,512]{1,0:T(8,128)(2,1)S(1)} collective-permute-done((bf16[144,512]{1,0:T(8,128)(2,1)S(1)}, bf16[144,512]{1,0:T(8,128)(2,1)S(1)}, u32[]{:S(2)}, u32[]{:S(2)}) %collective-permute-start.8) | collective-permute-done | bytes 147488 | tf_op jit(solution)/shard_map/ppermute | solution.py:19
  25.4 1.6 %collective-permute-start.9 = (bf16[4,128,512]{2,1,0:T(8,128)(2,1)S(1)}, bf16[4,128,512]{2,1,0:T(8,128)(2,1)S(1)}, u32[]{:S(2)}, u32[]{:S(2)}) collective-permute-start(bf16[4,128,512]{2,1,0:T(8,128)(2,1)S(1)} %pad_maximum_fusion.refs_8_), channel_id=1, source_target_pairs={{0,4},{4,0},{1,5},{5,1},{2,6},{6,2},{3,7},{7,3},{8,12},{12,8},{9,1... | collective-permute-start | bytes 1572872 | tf_op jit(solution)/shard_map/ppermute | solution.py:19
  28.0 1.7 %convolution_convert_fusion.1 = bf16[16,64,352]{2,1,0:T(8,128)(2,1)S(1)} fusion(bf16[16,64,512]{2,1,0:T(8,128)(2,1)S(1)} %get-tuple-element.65.placed, bf16[16,512,352]{1,2,0:T(8,128)(2,1)S(1)} %bitcast.40), kind=kOutput, calls=%fused_computation.1 | convolution fusion | flops 369459200 | bytes 7536640 | tf_op jit(solution)/shard_map/esd,ehd->esh/dot_general | solution.py:251
  29.8 1.7 %convolution_convert_fusion.2 = bf16[16,64,352]{2,1,0:T(8,128)(2,1)S(1)} fusion(bf16[16,64,512]{2,1,0:T(8,128)(2,1)S(1)} %get-tuple-element.65.placed, bf16[16,512,352]{1,2,0:T(8,128)(2,1)S(1)} %bitcast.45), kind=kOutput, calls=%fused_computation.2 | convolution fusion | flops 369459200 | bytes 7536640 | tf_op jit(solution)/shard_map/esd,ehd->esh/dot_general | solution.py:251
  34.9 3.9 %collective-permute-done.9.refs_4_ = bf16[4,128,512]{2,1,0:T(8,128)(2,1)S(1)} collective-permute-done((bf16[4,128,512]{2,1,0:T(8,128)(2,1)S(1)}, bf16[4,128,512]{2,1,0:T(8,128)(2,1)S(1)}, u32[]{:S(2)}, u32[]{:S(2)}) %collective-permute-start.9) | collective-permute-done | bytes 524320 | tf_op jit(solution)/shard_map/ppermute | solution.py:19
  40.2 1.7 %convolution_convert_fusion = bf16[16,64,352]{2,1,0:T(8,128)(2,1)S(1)} fusion(bf16[16,64,512]{2,1,0:T(8,128)(2,1)S(1)} %shard_map.86, bf16[16,512,352]{1,2,0:T(8,128)(2,1)S(1)} %bitcast.47), kind=kOutput, calls=%fused_computation | convolution fusion | flops 369459200 | bytes 7536640 | tf_op jit(solution)/shard_map/esd,ehd->esh/dot_general | solution.py:251
  43.0 1.7 %collective-permute-done.15 = bf16[2,16,16,352]{3,2,1,0:T(8,128)(2,1)S(1)} collective-permute-done((bf16[2,16,16,352]{3,2,1,0:T(8,128)(2,1)S(1)}, bf16[2,16,16,352]{3,2,1,0:T(8,128)(2,1)S(1)}, u32[]{:S(2)}, u32[]{:S(2)}) %collective-permute-start.15) | collective-permute-done | bytes 360480 | tf_op jit(solution)/shard_map/ppermute | solution.py:19
  46.4 4.8 %collective-permute-done.16 = bf16[16,16,352]{2,1,0:T(8,128)(2,1)S(1)} collective-permute-done((bf16[16,16,352]{2,1,0:T(8,128)(2,1)S(1)}, bf16[16,16,352]{2,1,0:T(8,128)(2,1)S(1)}, u32[]{:S(2)}, u32[]{:S(2)}) %collective-permute-start.16) | collective-permute-done | bytes 180256 | tf_op jit(solution)/shard_map/ppermute | solution.py:19
  54.2 5.0 %shard_map.87 = (bf16[128,512]{1,0:T(8,128)(2,1)S(1)}, bf16[128,512]{1,0:T(8,128)(2,1)S(1)}, bf16[128,512]{1,0:T(8,128)(2,1)S(1)}, bf16[128,512]{1,0:T(8,128)(2,1)S(1)}) custom-call(s32[4,8,256]{2,1,0:T(8,128)S(1)} %get-tuple-element.54.refs_5_.refs_0_.refs_1_, bf16[16,16,704]{2,1,0:T(8,128)(2,1)S(1)} %pad_maximum_fusion.1.refs_1_.h0, ...), custom_call_target="tpu_custom_call" | custom-call | flops 1476395008 | bytes 11534336 | tf_op jit(solution)/shard_map/pallas_call | solution.py:152
  60.7 2.6 %shard_map.88.refs_0_ = bf16[2,96,512]{2,1,0:T(8,128)(2,1)S(1)} custom-call(bf16[6,16,704]{2,1,0:T(8,128)(2,1)S(1)} %collective-permute-done.19.refs_0_, bf16[6,16,704]{2,1,0:T(8,128)(2,1)S(1)} %collective-permute-done.21.refs_1_, bf16[16,352,512]{2,1,0:T(8,128)(2,1)} %bitcast.42, bf16[16,352,512]{2,1,0:T(8,128)(2,1)} %bitcast.37), custom_call_target="tpu_custom_call" | custom-call | flops 34603008 | bytes 512 | tf_op jit(solution)/shard_map/pallas_call | solution.py:152
  65.5 3.8 %shard_map.89 = (bf16[128,512]{1,0:T(8,128)(2,1)S(1)}, bf16[128,512]{1,0:T(8,128)(2,1)S(1)}, bf16[128,512]{1,0:T(8,128)(2,1)S(1)}, bf16[128,512]{1,0:T(8,128)(2,1)S(1)}) custom-call(bf16[2,96,512]{2,1,0:T(8,128)(2,1)S(1)} %shard_map.88.refs_0_, s32[4,8,256]{2,1,0:T(8,128)S(1)} %get-tuple-element.54.refs_5_.refs_0_.refs_1_, ...), custom_call_target="tpu_custom_call" | custom-call | flops 922746880 | bytes 7208960 | tf_op jit(solution)/shard_map/pallas_call | solution.py:152
  71.4 1.6 %collective-permute-start.32 = (bf16[128,512]{1,0:T(8,128)(2,1)S(1)}, bf16[128,512]{1,0:T(8,128)(2,1)S(1)}, u32[]{:S(2)}, u32[]{:S(2)}) collective-permute-start(bf16[128,512]{1,0:T(8,128)(2,1)S(1)} %broadcast_select_fusion), channel_id=1, source_target_pairs={{0,1},{1,0},{2,3},{3,2},{4,5},{5,4},{6,7},{7,6},{8,9},{9,8},{10,11... | collective-permute-start | bytes 393224 | tf_op jit(solution)/shard_map/ppermute | solution.py:19
  75.3 1.7 %collective-permute-start.27 = (bf16[128,512]{1,0:T(8,128)(2,1)S(1)}, bf16[128,512]{1,0:T(8,128)(2,1)S(1)}, u32[]{:S(2)}, u32[]{:S(2)}) collective-permute-start(bf16[128,512]{1,0:T(8,128)(2,1)S(1)} %get-tuple-element.64), channel_id=1, source_target_pairs={{0,28},{4,24},{8,20},{12,16},{16,12},{20,8},{24,4},{28,0},{1,29},{... | collective-permute-start | bytes 393224 | tf_op jit(solution)/shard_map/ppermute | solution.py:233
  77.1 5.8 %shard_map.90 = (bf16[16,352,512]{2,1,0:T(8,128)(2,1)}, bf16[16,352,512]{2,1,0:T(8,128)(2,1)}) custom-call(bf16[16,64,512]{2,1,0:T(8,128)(2,1)S(1)} %get-tuple-element.65.placed, bf16[16,16,704]{2,1,0:T(8,128)(2,1)S(1)} %pad_maximum_fusion.1.refs_1_.h0, bf16[16,16,704]{2,1,0:T(8,128)(2,1)S(1)} %collective-permute-done.20.refs_2_.h1, ...), custom_call_target="tpu_custom_call" | custom-call | flops 2952790016 | bytes 11534336 | tf_op jit(solution)/shard_map/pallas_call | solution.py:183
  83.6 1.8 %collective-permute-start.28 = (bf16[128,512]{1,0:T(8,128)(2,1)S(1)}, bf16[128,512]{1,0:T(8,128)(2,1)S(1)}, u32[]{:S(2)}, u32[]{:S(2)}) collective-permute-start(bf16[128,512]{1,0:T(8,128)(2,1)S(1)} %broadcast_select_fusion.2), channel_id=1, source_target_pairs={{0,1},{1,0},{2,3},{3,2},{4,5},{5,4},{6,7},{7,6},{8,9},{9,8},{10,11... | collective-permute-start | bytes 393224 | tf_op jit(solution)/shard_map/ppermute | solution.py:19
  85.4 4.4 %collective-permute-done.28 = bf16[128,512]{1,0:T(8,128)(2,1)S(1)} collective-permute-done((bf16[128,512]{1,0:T(8,128)(2,1)S(1)}, bf16[128,512]{1,0:T(8,128)(2,1)S(1)}, u32[]{:S(2)}, u32[]{:S(2)}) %collective-permute-start.28) | collective-permute-done | bytes 131104 | tf_op jit(solution)/shard_map/ppermute | solution.py:19
  90.1 2.7 %collective-permute-start.33 = (bf16[128,512]{1,0:T(8,128)(2,1)S(1)}, bf16[128,512]{1,0:T(8,128)(2,1)S(1)}, u32[]{:S(2)}, u32[]{:S(2)}) collective-permute-start(bf16[128,512]{1,0:T(8,128)(2,1)S(1)} %get-tuple-element.79), channel_id=1, source_target_pairs={{0,2},{1,3},{2,0},{3,1},{4,6},{5,7},{6,4},{7,5},{8,10},{9,11},{10,... | collective-permute-start | bytes 393224 | tf_op jit(solution)/shard_map/ppermute | solution.py:19
  92.7 6.3 %collective-permute-done.33 = bf16[128,512]{1,0:T(8,128)(2,1)S(1)} collective-permute-done((bf16[128,512]{1,0:T(8,128)(2,1)S(1)}, bf16[128,512]{1,0:T(8,128)(2,1)S(1)}, u32[]{:S(2)}, u32[]{:S(2)}) %collective-permute-start.33) | collective-permute-done | bytes 131104 | tf_op jit(solution)/shard_map/ppermute | solution.py:19
  (102 shorter events, 28.9 us)
Async XLA Ops:
  3.4 6.7 %collective-permute-start.1 = (bf16[144,512]{1,0:T(8,128)(2,1)S(1)}, bf16[144,512]{1,0:T(8,128)(2,1)S(1)}, u32[]{:S(2)}, u32[]{:S(2)}) collective-permute-start(bf16[144,512]{1,0:T(8,128)(2,1)S(1)} %get-tuple-element.98), channel_id=1, source_target_pairs={{0,24},{4,28},{8,16},{12,20},{16,8},{20,12},{24,0},{28,4},{1,25},{... | collective-permute-start | bytes 442376 | tf_op jit(solution)/shard_map/ppermute | solution.py:233
  5.9 7.6 %collective-permute-start = (bf16[144,512]{1,0:T(8,128)(2,1)S(1)}, bf16[144,512]{1,0:T(8,128)(2,1)S(1)}, u32[]{:S(2)}, u32[]{:S(2)}) collective-permute-start(bf16[144,512]{1,0:T(8,128)(2,1)S(1)} %get-tuple-element.101), channel_id=1, source_target_pairs={{0,16},{4,20},{8,24},{12,28},{16,0},{20,4},{24,8},{28,12},{1,17},{... | collective-permute-start | bytes 442376 | tf_op jit(solution)/shard_map/ppermute | solution.py:233
  6.5 9.4 %collective-permute-start.5 = (bf16[144,512]{1,0:T(8,128)(2,1)S(1)}, bf16[144,512]{1,0:T(8,128)(2,1)S(1)}, u32[]{:S(2)}, u32[]{:S(2)}) collective-permute-start(bf16[144,512]{1,0:T(8,128)(2,1)S(1)} %get-tuple-element.99.refs_0_), channel_id=1, source_target_pairs={{0,4},{4,0},{8,12},{12,8},{16,20},{20,16},{24,28},{28,24},{1,5},{5... | collective-permute-start | bytes 442376 | tf_op jit(solution)/shard_map/ppermute | solution.py:233
  8.0 8.0 %collective-permute-start.6 = (bf16[144,512]{1,0:T(8,128)(2,1)S(1)}, bf16[144,512]{1,0:T(8,128)(2,1)S(1)}, u32[]{:S(2)}, u32[]{:S(2)}) collective-permute-start(bf16[144,512]{1,0:T(8,128)(2,1)S(1)} %get-tuple-element.100), channel_id=1, source_target_pairs={{0,12},{4,8},{8,4},{12,0},{16,28},{20,24},{24,20},{28,16},{1,13},{... | collective-permute-start | bytes 442376 | tf_op jit(solution)/shard_map/ppermute | solution.py:233
  13.4 6.7 %collective-permute-start.3 = (bf16[128,512]{1,0:T(8,128)(2,1)S(1)}, bf16[128,512]{1,0:T(8,128)(2,1)S(1)}, u32[]{:S(2)}, u32[]{:S(2)}) collective-permute-start(bf16[128,512]{1,0:T(8,128)(2,1)S(1)} %get-tuple-element.43), channel_id=1, source_target_pairs={{0,16},{4,20},{8,24},{12,28},{16,0},{20,4},{24,8},{28,12},{1,17},{... | collective-permute-start | bytes 393224 | tf_op jit(solution)/shard_map/ppermute | solution.py:233
  15.8 6.6 %collective-permute-start.4 = (bf16[128,512]{1,0:T(8,128)(2,1)S(1)}, bf16[128,512]{1,0:T(8,128)(2,1)S(1)}, u32[]{:S(2)}, u32[]{:S(2)}) collective-permute-start(bf16[128,512]{1,0:T(8,128)(2,1)S(1)} %get-tuple-element.44), channel_id=1, source_target_pairs={{0,24},{4,28},{8,16},{12,20},{16,8},{20,12},{24,0},{28,4},{1,25},{... | collective-permute-start | bytes 393224 | tf_op jit(solution)/shard_map/ppermute | solution.py:233
  15.9 11.1 %collective-permute-start.10 = (bf16[144,512]{1,0:T(8,128)(2,1)S(1)}, bf16[144,512]{1,0:T(8,128)(2,1)S(1)}, u32[]{:S(2)}, u32[]{:S(2)}) collective-permute-start(bf16[144,512]{1,0:T(8,128)(2,1)S(1)} %get-tuple-element.100), channel_id=1, source_target_pairs={{0,8},{4,12},{8,0},{12,4},{16,24},{20,28},{24,16},{28,20},{1,9},{5... | collective-permute-start | bytes 442376 | tf_op jit(solution)/shard_map/ppermute | solution.py:233
  16.0 6.7 %collective-permute-start.7 = (bf16[144,512]{1,0:T(8,128)(2,1)S(1)}, bf16[144,512]{1,0:T(8,128)(2,1)S(1)}, u32[]{:S(2)}, u32[]{:S(2)}) collective-permute-start(bf16[144,512]{1,0:T(8,128)(2,1)S(1)} %collective-permute-done.refs_2_), channel_id=1, source_target_pairs={{0,4},{4,0},{1,5},{5,1},{2,6},{6,2},{3,7},{7,3},{8,12},{12,8},{9,1... | collective-permute-start | bytes 442376 | tf_op jit(solution)/shard_map/ppermute | solution.py:19
  17.9 7.5 %collective-permute-start.8 = (bf16[144,512]{1,0:T(8,128)(2,1)S(1)}, bf16[144,512]{1,0:T(8,128)(2,1)S(1)}, u32[]{:S(2)}, u32[]{:S(2)}) collective-permute-start(bf16[144,512]{1,0:T(8,128)(2,1)S(1)} %collective-permute-done.1.refs_3_), channel_id=1, source_target_pairs={{0,4},{4,0},{1,5},{5,1},{2,6},{6,2},{3,7},{7,3},{8,12},{12,8},{9,1... | collective-permute-start | bytes 442376 | tf_op jit(solution)/shard_map/ppermute | solution.py:19
  25.4 13.5 %collective-permute-start.9 = (bf16[4,128,512]{2,1,0:T(8,128)(2,1)S(1)}, bf16[4,128,512]{2,1,0:T(8,128)(2,1)S(1)}, u32[]{:S(2)}, u32[]{:S(2)}) collective-permute-start(bf16[4,128,512]{2,1,0:T(8,128)(2,1)S(1)} %pad_maximum_fusion.refs_8_), channel_id=1, source_target_pairs={{0,4},{4,0},{1,5},{5,1},{2,6},{6,2},{3,7},{7,3},{8,12},{12,8},{9,1... | collective-permute-start | bytes 1572872 | tf_op jit(solution)/shard_map/ppermute | solution.py:19
  33.3 11.5 %collective-permute-start.15 = (bf16[2,16,16,352]{3,2,1,0:T(8,128)(2,1)S(1)}, bf16[2,16,16,352]{3,2,1,0:T(8,128)(2,1)S(1)}, u32[]{:S(2)}, u32[]{:S(2)}) collective-permute-start(bf16[2,16,16,352]{3,2,1,0:T(8,128)(2,1)S(1)} %pad_maximum_fusion.2.refs_6_), channel_id=1, source_target_pairs={{0,16},{8,24},{16,0},{24,8},{1,17},{9,25},{17,1},{25,9},{2,18},{10... | collective-permute-start | bytes 1081352 | tf_op jit(solution)/shard_map/ppermute | solution.py:19
  44.8 6.4 %collective-permute-start.16 = (bf16[16,16,352]{2,1,0:T(8,128)(2,1)S(1)}, bf16[16,16,352]{2,1,0:T(8,128)(2,1)S(1)}, u32[]{:S(2)}, u32[]{:S(2)}) collective-permute-start(bf16[16,16,352]{2,1,0:T(8,128)(2,1)S(1)} %add_convert_fusion), channel_id=1, source_target_pairs={{0,16},{8,24},{16,0},{24,8},{1,17},{9,25},{17,1},{25,9},{2,18},{10... | collective-permute-start | bytes 540680 | tf_op jit(solution)/shard_map/ppermute | solution.py:19
  52.0 7.3 %collective-permute-start.19 = (bf16[6,16,704]{2,1,0:T(8,128)(2,1)S(1)}, bf16[6,16,704]{2,1,0:T(8,128)(2,1)S(1)}, u32[]{:S(2)}, u32[]{:S(2)}) collective-permute-start(bf16[6,16,704]{2,1,0:T(8,128)(2,1)S(1)} %fusion.7), channel_id=1, source_target_pairs={{0,16},{8,24},{16,0},{24,8},{1,17},{9,25},{17,1},{25,9},{2,18},{10... | collective-permute-start | bytes 405512 | tf_op jit(solution)/shard_map/ppermute | solution.py:19
  53.7 9.9 %collective-permute-start.22 = (bf16[10,16,704]{2,1,0:T(8,128)(2,1)S(1)}, bf16[10,16,704]{2,1,0:T(8,128)(2,1)S(1)}, u32[]{:S(2)}, u32[]{:S(2)}) collective-permute-start(bf16[10,16,704]{2,1,0:T(8,128)(2,1)S(1)} %fusion.4), channel_id=1, source_target_pairs={{0,16},{8,24},{16,0},{24,8},{1,17},{9,25},{17,1},{25,9},{2,18},{10... | collective-permute-start | bytes 675848 | tf_op jit(solution)/shard_map/ppermute | solution.py:19
  63.6 7.3 %collective-permute-start.29 = (bf16[128,512]{1,0:T(8,128)(2,1)S(1)}, bf16[128,512]{1,0:T(8,128)(2,1)S(1)}, u32[]{:S(2)}, u32[]{:S(2)}) collective-permute-start(bf16[128,512]{1,0:T(8,128)(2,1)S(1)} %get-tuple-element.72), channel_id=1, source_target_pairs={{0,8},{4,12},{8,0},{12,4},{16,24},{20,28},{24,16},{28,20},{1,9},{5... | collective-permute-start | bytes 393224 | tf_op jit(solution)/shard_map/ppermute | solution.py:233
  64.0 6.8 %collective-permute-start.30 = (bf16[128,512]{1,0:T(8,128)(2,1)S(1)}, bf16[128,512]{1,0:T(8,128)(2,1)S(1)}, u32[]{:S(2)}, u32[]{:S(2)}) collective-permute-start(bf16[128,512]{1,0:T(8,128)(2,1)S(1)} %get-tuple-element.73), channel_id=1, source_target_pairs={{0,4},{4,0},{8,12},{12,8},{16,20},{20,16},{24,28},{28,24},{1,5},{5... | collective-permute-start | bytes 393224 | tf_op jit(solution)/shard_map/ppermute | solution.py:233
  64.7 6.7 %collective-permute-start.31 = (bf16[128,512]{1,0:T(8,128)(2,1)S(1)}, bf16[128,512]{1,0:T(8,128)(2,1)S(1)}, u32[]{:S(2)}, u32[]{:S(2)}) collective-permute-start(bf16[128,512]{1,0:T(8,128)(2,1)S(1)} %get-tuple-element.74), channel_id=1, source_target_pairs={{0,12},{4,8},{8,4},{12,0},{16,28},{20,24},{24,20},{28,16},{1,13},{... | collective-permute-start | bytes 393224 | tf_op jit(solution)/shard_map/ppermute | solution.py:233
  69.3 14.3 %collective-permute-start.24 = (bf16[128,512]{1,0:T(8,128)(2,1)S(1)}, bf16[128,512]{1,0:T(8,128)(2,1)S(1)}, u32[]{:S(2)}, u32[]{:S(2)}) collective-permute-start(bf16[128,512]{1,0:T(8,128)(2,1)S(1)} %get-tuple-element.61), channel_id=1, source_target_pairs={{0,16},{4,20},{8,24},{12,28},{16,0},{20,4},{24,8},{28,12},{1,17},{... | collective-permute-start | bytes 393224 | tf_op jit(solution)/shard_map/ppermute | solution.py:233
  71.4 14.0 %collective-permute-start.32 = (bf16[128,512]{1,0:T(8,128)(2,1)S(1)}, bf16[128,512]{1,0:T(8,128)(2,1)S(1)}, u32[]{:S(2)}, u32[]{:S(2)}) collective-permute-start(bf16[128,512]{1,0:T(8,128)(2,1)S(1)} %broadcast_select_fusion), channel_id=1, source_target_pairs={{0,1},{1,0},{2,3},{3,2},{4,5},{5,4},{6,7},{7,6},{8,9},{9,8},{10,11... | collective-permute-start | bytes 393224 | tf_op jit(solution)/shard_map/ppermute | solution.py:19
  73.1 10.5 %collective-permute-start.25 = (bf16[128,512]{1,0:T(8,128)(2,1)S(1)}, bf16[128,512]{1,0:T(8,128)(2,1)S(1)}, u32[]{:S(2)}, u32[]{:S(2)}) collective-permute-start(bf16[128,512]{1,0:T(8,128)(2,1)S(1)} %get-tuple-element.62), channel_id=1, source_target_pairs={{0,24},{4,28},{8,16},{12,20},{16,8},{20,12},{24,0},{28,4},{1,25},{... | collective-permute-start | bytes 393224 | tf_op jit(solution)/shard_map/ppermute | solution.py:233
  74.7 8.9 %collective-permute-start.26 = (bf16[128,512]{1,0:T(8,128)(2,1)S(1)}, bf16[128,512]{1,0:T(8,128)(2,1)S(1)}, u32[]{:S(2)}, u32[]{:S(2)}) collective-permute-start(bf16[128,512]{1,0:T(8,128)(2,1)S(1)} %get-tuple-element.63), channel_id=1, source_target_pairs={{0,20},{4,16},{8,28},{12,24},{16,4},{20,0},{24,12},{28,8},{1,21},{... | collective-permute-start | bytes 393224 | tf_op jit(solution)/shard_map/ppermute | solution.py:233
  75.3 8.3 %collective-permute-start.27 = (bf16[128,512]{1,0:T(8,128)(2,1)S(1)}, bf16[128,512]{1,0:T(8,128)(2,1)S(1)}, u32[]{:S(2)}, u32[]{:S(2)}) collective-permute-start(bf16[128,512]{1,0:T(8,128)(2,1)S(1)} %get-tuple-element.64), channel_id=1, source_target_pairs={{0,28},{4,24},{8,20},{12,16},{16,12},{20,8},{24,4},{28,0},{1,29},{... | collective-permute-start | bytes 393224 | tf_op jit(solution)/shard_map/ppermute | solution.py:233
  83.6 6.2 %collective-permute-start.28 = (bf16[128,512]{1,0:T(8,128)(2,1)S(1)}, bf16[128,512]{1,0:T(8,128)(2,1)S(1)}, u32[]{:S(2)}, u32[]{:S(2)}) collective-permute-start(bf16[128,512]{1,0:T(8,128)(2,1)S(1)} %broadcast_select_fusion.2), channel_id=1, source_target_pairs={{0,1},{1,0},{2,3},{3,2},{4,5},{5,4},{6,7},{7,6},{8,9},{9,8},{10,11... | collective-permute-start | bytes 393224 | tf_op jit(solution)/shard_map/ppermute | solution.py:19
  90.1 9.0 %collective-permute-start.33 = (bf16[128,512]{1,0:T(8,128)(2,1)S(1)}, bf16[128,512]{1,0:T(8,128)(2,1)S(1)}, u32[]{:S(2)}, u32[]{:S(2)}) collective-permute-start(bf16[128,512]{1,0:T(8,128)(2,1)S(1)} %get-tuple-element.79), channel_id=1, source_target_pairs={{0,2},{1,3},{2,0},{3,1},{4,6},{5,7},{6,4},{7,5},{8,10},{9,11},{10,... | collective-permute-start | bytes 393224 | tf_op jit(solution)/shard_map/ppermute | solution.py:19
  (20 other events, 98.0 us)
